TPU v7x, 256 devices: a whole 4x4x8 slice. The times are simulated.
256 devices in a mesh: rep: 32 (over y, x, core), shard: 8 (over z).
Axes of the slice: x: 4, y: 4, z: 8, core: 2. Of those that a mesh axis runs over, the one named last changes fastest.
Arguments:
- grads: bfloat16 [32, 1024, 8192], P('rep', 'shard'), may hold values from -6 to 6
- errors: bfloat16 [32, 1024, 8192], P('rep', 'shard'), may hold values from -4 to 4
- q_prev: float32 [8192, 128], P('shard'), may hold values from -0.0625 to 0.0625
- moment: float32 [1024, 8192], P('shard'), may hold values from -0.12 to 0.12
- second: float32 [1024, 8192], P('shard'), may hold values from 0.0001 to 0.01
Outputs:
- errors_next: bfloat16 [32, 1024, 8192], P('rep', 'shard')
- q_next: float32 [8192, 128], P('shard')
- moment_next: float32 [1024, 8192], P('shard')
- second_next: float32 [1024, 8192], P('shard')
- update: bfloat16 [1024, 8192], P('shard')
All inputs are finite; a program needn't handle non-finite values.
Results may differ from a plain program's by a relative error of at most 0.0012.
Values sent between devices are 32-bit elements; how exact they have to be, the bound alone decides.
No kernel may reach another device: no remote copies, remote signals or barrier semaphores. Data moves between devices by JAX's collectives and lax.ppermute only.
A program may use at most 128 MiB of HBM per device.

v0:
```python
import functools

import jax
import jax.numpy as jnp
from jax import lax
from jax.experimental import pallas as pl
from jax.experimental.pallas import tpu as pltpu
from jax.sharding import Mesh, PartitionSpec as P

ADAM_STEP = 10
HI = lax.Precision.HIGHEST
F32 = jnp.float32
ALL = ("y", "x", "core", "z")
REPS = 32


def vmem():
    return pl.BlockSpec(memory_space=pltpu.VMEM)


def params(mib=16):
    return pltpu.CompilerParams(vmem_limit_bytes=mib * 1024 * 1024)


def split(value):
    high = value.astype(jnp.bfloat16)
    rest = value - high.astype(F32)
    middle = rest.astype(jnp.bfloat16)
    return high, middle, (rest - middle.astype(F32)).astype(jnp.bfloat16)


def short_nt(a, b):
    return lax.dot_general(a, b, (((1,), (1,)), ((), ())), preferred_element_type=F32)


def dot_nt(a, b):
    return lax.dot_general(a, b, (((1,), (1,)), ((), ())), precision=HI, preferred_element_type=F32)


def merge_half(place, other, grads, errors):
    rows, cols = grads.shape
    wide = cols // 8
    thin = wide // 4

    def body(at, g, e, *outs):
        core = 1 - at[0] if other else at[0]
        for k in range(4):
            for j in range(4):
                block = core * 16 + (at[1] + k) % 4 * 4 + (at[2] + j) % 4
                block = pl.ds(pl.multiple_of(block * thin, thin), thin)
                value = g[:, block].astype(F32) + e[:, block].astype(F32)
                outs[k][:, j * thin : (j + 1) * thin] = value

    return pl.pallas_call(
        body,
        in_specs=[pl.BlockSpec(memory_space=pltpu.SMEM)] + [vmem()] * 2,
        out_specs=[vmem()] * 4,
        out_shape=[jax.ShapeDtypeStruct((rows, wide), F32)] * 4,
        compiler_params=params(),
        name="merge_half",
    )(place, grads, errors)


def sum_split(parts):
    rows, wide = parts[0].shape
    thin = wide // 4
    count = len(parts)

    def body(*refs):
        for k in range(4):
            value = refs[0][:, k * thin : (k + 1) * thin]
            for ref in refs[1:count]:
                value = value + ref[:, k * thin : (k + 1) * thin]
            refs[count + k][...] = value

    return pl.pallas_call(
        body,
        in_specs=[vmem()] * count,
        out_specs=[vmem()] * 4,
        out_shape=[jax.ShapeDtypeStruct((rows, thin), F32)] * 4,
        compiler_params=params(),
        name="sum_split",
    )(*parts)


def left_part(parts, right):
    rows, cols = parts[0].shape

    def body(a, b, c, d, q, m_out, p_out):
        m_out[...] = (a[...] + b[...]) + (c[...] + d[...])
        p_out[...] = jnp.dot(m_out[...], q[...], precision=HI, preferred_element_type=F32)

    return pl.pallas_call(
        body,
        in_specs=[vmem()] * 5,
        out_specs=[vmem()] * 2,
        out_shape=[
            jax.ShapeDtypeStruct((rows, cols), F32),
            jax.ShapeDtypeStruct((rows, right.shape[1]), F32),
        ],
        compiler_params=params(),
        name="left_part",
    )(*parts, right)


def products(m, p):
    cols, rank = m.shape[1], p.shape[1]
    high, low = cols // 8, rank // 8

    def body(m_ref, p_ref, out):
        p_val = p_ref[...]
        t = jnp.dot(m_ref[...].T, p_val, precision=HI, preferred_element_type=F32)
        gram = jnp.dot(p_val.T, p_val, precision=HI, preferred_element_type=F32)
        out[:, :high, :] = t.reshape(8, high, rank)
        out[:, high:, :] = gram.reshape(8, low, rank)

    return pl.pallas_call(
        body,
        in_specs=[vmem()] * 2,
        out_specs=vmem(),
        out_shape=jax.ShapeDtypeStruct((8, high + low, rank), F32),
        compiler_params=params(),
        name="products",
    )(m, p)


def total(parts):
    def body(*refs):
        value = refs[0][...]
        for ref in refs[1:-1]:
            value = value + ref[...]
        refs[-1][...] = value

    return pl.pallas_call(
        body,
        in_specs=[vmem()] * len(parts),
        out_specs=vmem(),
        out_shape=jax.ShapeDtypeStruct(parts[0].shape, F32),
        compiler_params=params(),
        name="total",
    )(*parts)


def stack(parts):
    rows, cols = parts[0].shape

    def body(*refs):
        for i in range(len(parts)):
            refs[-1][i * rows : (i + 1) * rows, :] = refs[i][...]

    return pl.pallas_call(
        body,
        in_specs=[vmem()] * len(parts),
        out_specs=vmem(),
        out_shape=jax.ShapeDtypeStruct((len(parts) * rows, cols), F32),
        compiler_params=params(),
        name="stack",
    )(*parts)


def halves(a, b):
    rows, cols = a.shape[0] // 2, a.shape[1]

    def body(a_ref, b_ref, up, down):
        up[...] = a_ref[:rows]
        down[...] = b_ref[rows:]

    return pl.pallas_call(
        body,
        in_specs=[vmem()] * 2,
        out_specs=[vmem()] * 2,
        out_shape=[jax.ShapeDtypeStruct((rows, cols), F32)] * 2,
        compiler_params=params(),
        name="halves",
    )(a, b)


def sum_copies(parts):
    def body(a, out):
        value = jnp.sum(a[...], axis=0)
        out[...] = jnp.broadcast_to(value[None], out.shape)

    return pl.pallas_call(
        body,
        in_specs=[vmem()],
        out_specs=vmem(),
        out_shape=jax.ShapeDtypeStruct(parts.shape, F32),
        compiler_params=params(),
        name="sum_copies",
    )(parts)


def unpack(whole, high):
    count, both, rank = whole.shape
    low = both - high

    def body(a, t, gram):
        for i in range(count):
            t[i * high : (i + 1) * high, :] = a[i, :high, :]
            gram[i * low : (i + 1) * low, :] = a[i, high:, :]

    return pl.pallas_call(
        body,
        in_specs=[vmem()],
        out_specs=[vmem()] * 2,
        out_shape=[
            jax.ShapeDtypeStruct((count * high, rank), F32),
            jax.ShapeDtypeStruct((count * low, rank), F32),
        ],
        compiler_params=params(),
        name="unpack",
    )(whole)


def rows_of(place, q_prev):
    rows = q_prev.shape[0] // 4

    def body(at, q, out):
        out[...] = q[pl.ds(pl.multiple_of(at[2] * rows, rows), rows), :]

    return pl.pallas_call(
        body,
        in_specs=[pl.BlockSpec(memory_space=pltpu.SMEM), vmem()],
        out_specs=vmem(),
        out_shape=jax.ShapeDtypeStruct((rows, q_prev.shape[1]), F32),
        compiler_params=params(),
        name="rows_of",
    )(place, q_prev)


def choose(place, hits, came, have):
    def body(at, a, b, out):
        away = (at[3] + 8 - (at[0] * 4 + at[1])) % 8
        hit = functools.reduce(jnp.logical_or, [away == h for h in hits])
        out[...] = jnp.where(hit, a[...], b[...])

    return pl.pallas_call(
        body,
        in_specs=[pl.BlockSpec(memory_space=pltpu.SMEM)] + [vmem()] * 2,
        out_specs=vmem(),
        out_shape=jax.ShapeDtypeStruct(came.shape, F32),
        compiler_params=params(),
        name="choose",
    )(place, came, have)


ORDER = (0, 1, 3, 2)
UNIT = 8
STRIP = 16


def invert(gram, p):
    n = gram.shape[0]

    def unit(left, right, at):
        wide = (1, 2 * n)

        def element(i, j):
            return jnp.broadcast_to(left[i : i + 1, at + j : at + j + 1], wide)

        a = [[element(i, j) for j in range(i + 1)] for i in range(UNIT)]
        rows = [
            jnp.concatenate([left[i : i + 1, :], right[i : i + 1, :]], axis=1) for i in range(UNIT)
        ]
        for j in range(UNIT):
            scale = lax.rsqrt(a[j][j])
            rows[j] = rows[j] * scale
            col = [a[i][j] * scale for i in range(j + 1, UNIT)]
            for i in range(j + 1, UNIT):
                for k in range(j + 1, i + 1):
                    a[i][k] = a[i][k] - col[i - j - 1] * col[k - j - 1]
                rows[i] = rows[i] - col[i - j - 1] * rows[j]
        both = jnp.concatenate(rows, axis=0)
        return both[:, :n], both[:, n:]

    def body(g_ref, p_ref, inv_out, w_out, work):
        row = lax.broadcasted_iota(jnp.int32, (n, n), 0)
        col = lax.broadcasted_iota(jnp.int32, (n, n), 1)
        work[:, :n] = g_ref[...]
        work[:, n:] = jnp.where(row == col, 1.0, 0.0).astype(F32)
        for at in range(0, n, STRIP):
            mid, end = at + UNIT, at + STRIP
            left, right = unit(work[at:mid, :n], work[at:mid, n:], at)
            low_left, low_right = work[mid:end, :n], work[mid:end, n:]
            factors = left[:, mid:end].T
            for j in range(UNIT):
                factor = factors[:, j : j + 1]
                low_left = low_left - factor * left[j : j + 1, :]
                low_right = low_right - factor * right[j : j + 1, :]
            low_left, low_right = unit(low_left, low_right, mid)
            inv_out[at:mid, :] = right
            inv_out[mid:end, :] = low_right
            if end < n:
                strip = jnp.concatenate([left, low_left], axis=0)
                both = jnp.concatenate(
                    [strip, jnp.concatenate([right, low_right], axis=0)], axis=1
                )
                work[end:, :] -= lax.dot_general(
                    strip[:, end:],
                    both,
                    (((0,), (0,)), ((), ())),
                    precision=HI,
                    preferred_element_type=F32,
                )
        inv = inv_out[...]
        p_hat = dot_nt(p_ref[...], inv)
        weight = jnp.dot(p_hat, inv, precision=HI, preferred_element_type=F32) * (1.0 / REPS)
        high, middle, low = split(weight)
        for i, pair in enumerate(((high, high), (middle, middle), (low, high))):
            w_out[i * n : (i + 1) * n, :] = jnp.concatenate(pair, axis=1)

    return pl.pallas_call(
        body,
        in_specs=[vmem()] * 2,
        out_specs=[vmem()] * 2,
        out_shape=[jax.ShapeDtypeStruct((n, n), F32), jax.ShapeDtypeStruct((3 * n, 2 * n), jnp.bfloat16)],
        scratch_shapes=[pltpu.VMEM((n, 2 * n), F32)],
        compiler_params=params(),
        cost_estimate=pl.CostEstimate(flops=8 * 10**9, bytes_accessed=1 << 18, transcendentals=n),
        name="invert",
    )(gram, p)


def finish(place, which, ts, weight, merged, moment, second, before=(), extra=()):
    rows, cols = moment.shape
    count = len(ts)
    wide, rank = ts[0].shape
    thin = wide // 4
    fix_one = 1.0 / (1.0 - 0.9**ADAM_STEP)
    fix_two = 1.0 / (1.0 - 0.95**ADAM_STEP)
    tail = len(before) + len(extra)

    def body(at, *refs):
        blocks = refs[count : count + 8]
        w_ref, m, v = refs[count + 8 : count + 11]
        outs = refs[count + 11 + tail :]
        e_out, m_out, v_out, u_out = outs[:4]
        for i in range(count):

            @pl.when(pl.program_id(0) == i)
            def _(i=i):
                kc, kx = i % 2, (4 - i // 2 - which) % 4
                for j in range(4):
                    ky = (4 - j) % 4
                    block = pl.ds(pl.multiple_of(((at[2] + ky) % 4) * thin, thin), thin)
                    t = refs[i][j * thin : (j + 1) * thin, :]
                    high, middle, low = split(t)
                    big = short_nt(w_ref[: 2 * rows, :], jnp.concatenate([high, middle], axis=1))
                    small = short_nt(w_ref[2 * rows :, :], jnp.concatenate([high, low], axis=1))
                    approx = big[:rows] + (big[rows:] + small)
                    full = blocks[4 * kc + kx][:, ky * thin : (ky + 1) * thin]
                    e_out[:, block] = (full - approx).astype(jnp.bfloat16)
                    core = at[0] if kc == 0 else 1 - at[0]
                    place = (core * 4 + (at[1] + kx) % 4) * 4 + (at[2] + ky) % 4
                    place = pl.ds(pl.multiple_of(place * thin, thin), thin)
                    m_next = 0.9 * m[:, place] + 0.1 * approx
                    v_next = 0.95 * v[:, place] + 0.05 * approx * approx
                    m_out[:, block] = m_next
                    v_out[:, block] = v_next
                    root = v_next * fix_two
                    root = root * lax.rsqrt(root)
                    u_out[:, block] = ((m_next * fix_one) / (root + 1e-08)).astype(jnp.bfloat16)

        if extra:
            inv = refs[count + 11 + tail - 1]
            near = refs[count + 11 + 4 : count + 11 + tail - 1]
            for i, t in enumerate((*near, *refs[:count])):
                core = at[0] if i % 2 == 0 else 1 - at[0]
                owner = core * 4 + (at[1] + 4 - ORDER[i // 2]) % 4

                @pl.when(jnp.logical_and(pl.program_id(0) == 0, owner == at[3]))
                def _(t=t):
                    for j in range(4):
                        part = pl.ds(pl.multiple_of(((at[2] + 4 - j) % 4) * thin, thin), thin)
                        value = dot_nt(t[j * thin : (j + 1) * thin, :], inv[...])
                        outs[4][part, :] = value * (1.0 / REPS)

    def column(i, at):
        kc, kx = i % 2, i // 2 + which
        core = at[0] + kc - 2 * at[0] * kc
        return (0, core * 4 + (at[1] + 4 - kx) % 4)

    block = pl.BlockSpec((rows, wide), column)
    ins = [vmem()] * (count + 11)
    args = [place, *ts, *merged, weight, moment, second]
    specs = [block] * 4
    shapes = [
        jax.ShapeDtypeStruct((rows, cols), d) for d in (jnp.bfloat16, F32, F32, jnp.bfloat16)
    ]
    alias = {len(args) + i: i for i in range(len(before))}
    ins += [pl.BlockSpec(memory_space=pl.ANY)] * len(before) + [vmem()] * len(extra)
    args += [*before, *extra]
    if extra:
        specs.append(vmem())
        shapes.append(jax.ShapeDtypeStruct((wide, rank), F32))
    return pl.pallas_call(
        body,
        grid_spec=pltpu.PrefetchScalarGridSpec(
            num_scalar_prefetch=1, grid=(count,), in_specs=ins, out_specs=specs
        ),
        out_shape=shapes,
        input_output_aliases=alias,
        compiler_params=params(28),
        name="finish",
    )(*args)


def shift(value, axis, step):
    n = lax.axis_size(axis)
    return lax.ppermute(value, axis, [(i, (i + step) % n) for i in range(n)])


def device(y, x, core, z):
    return ((y * 4 + x) * 2 + core) * 8 + z


def spread(block, steps, held):
    pairs = []
    for y in range(4):
        for x in range(4):
            for core in range(2):
                for h in held:
                    z = (core * 4 + x + h) % 8
                    pairs.append((device(y, x, core, z), device(y, x, core, (z + steps) % 8)))
    return lax.ppermute(block, ALL, pairs)


def on_device(grads, errors, q_prev, moment, second):
    y, x, core, z = (lax.axis_index(a) for a in ALL)
    place = jnp.stack([core, x, y, z]).astype(jnp.int32)
    grads, errors = grads[0], errors[0]

    theirs = merge_half(place, True, grads, errors)
    came = {k: shift(theirs[k], "core", 1) for k in (1, 2, 3, 0)}
    mine = merge_half(place, False, grads, errors)
    merged = [*mine, *theirs]

    right = rows_of(place, q_prev)
    held = [0]
    for step in (4, 2, 1):
        new = [h + step for h in held]
        right = choose(place, new, spread(right, step, held), right)
        held = held + new

    parts = [shift(total([mine[k], came[k]]), "x", k) for k in (1, 2, 3)]
    blocks = sum_split([mine[0], came[0], *parts])
    m, p = left_part([blocks[0]] + [shift(blocks[k], "y", k) for k in (1, 2, 3)], right)

    for axis in ("x", "y"):
        p = total([p] + [shift(p, axis, k) for k in (1, 2, 3)])
    p = total([p, shift(p, "core", 1)])

    whole = lax.all_to_all(products(m, p), "z", 0, 0)
    whole = lax.all_to_all(sum_copies(whole), "z", 0, 0)
    t, gram = unpack(whole, m.shape[1] // 8)
    t = stack([t] + [shift(t, "y", k) for k in (1, 2, 3)])
    t, gram = lax.optimization_barrier((t, gram))
    def pair(block):
        return [block, shift(block, "core", 1)]

    near = pair(t)
    one, three = shift(t, "x", 1), shift(t, "x", 3)
    inverse, weight = invert(gram, p)
    out = finish(place, 0, near, weight, merged, moment, second)
    out, one, three = lax.optimization_barrier((out, one, three))

    upper, lower = halves(one, three)
    two = [shift(upper, "x", 1), shift(lower, "x", 3)]
    one, three = pair(one), pair(three)
    out = finish(place, 1, one, weight, merged, moment, second, out)
    out = finish(place, 3, three, weight, merged, moment, second, out)
    out, two = lax.optimization_barrier((out, two))
    two = pair(stack(two))
    e_next, m_next, v_next, update, q_next = finish(
        place, 2, two, weight, merged, moment, second, out, [*near, *one, *three, inverse]
    )
    return (e_next[None], q_next, m_next, v_next, update)


def solution(mesh):
    grid = Mesh(mesh.devices.reshape(4, 4, 2, 8), ALL)
    rep = ("y", "x", "core")
    return jax.shard_map(
        on_device,
        mesh=grid,
        in_specs=(P(rep, "z", None), P(rep, "z", None), P("z", None), P("z", None), P("z", None)),
        out_specs=(P(rep, "z", None), P("z", None), P("z", None), P("z", None), P("z", None)),
        check_vma=False,
    )
```

profile of v0, /device:TPU:1, one launch (start us, length us, event | category | flops | bytes accessed | tf_op | source)
XLA Modules:
  0.0 136.1 jit_solution(4710990002954703815)
XLA Ops:
  0.7 1.6 %copy-done.2 = bf16[1,128,8192]{2,1,0:T(8,128)(2,1)S(1)} copy-done((bf16[1,128,8192]{2,1,0:T(8,128)(2,1)S(1)}, bf16[1,128,8192]{2,1,0:T(8,128)(2,1)}, u32[]{:S(2)}) %copy-start.2) | copy-done | bytes 2097176
  2.3 1.6 %copy-done.3 = bf16[1,128,8192]{2,1,0:T(8,128)(2,1)S(1)} copy-done((bf16[1,128,8192]{2,1,0:T(8,128)(2,1)S(1)}, bf16[1,128,8192]{2,1,0:T(8,128)(2,1)}, u32[]{:S(2)}) %copy-start.3) | copy-done | bytes 2097176
  4.7 3.3 %collective-permute-start.5 = (f32[128,1024]{1,0:T(8,128)S(1)}, f32[128,1024]{1,0:T(8,128)S(1)}, u32[]{:S(2)}, u32[]{:S(2)}) collective-permute-start(f32[128,1024]{1,0:T(8,128)S(1)} %get-tuple-element.63.refs_9_), channel_id=1, source_target_pairs={{0,8},{8,0},{1,9},{9,1},{2,10},{10,2},{3,11},{11,3},{4,12},{12,4},... | collective-permute-start | bytes 1572872 | tf_op jit(solution)/shard_map/ppermute | solution.py:410
  12.5 1.3 collective-permute-start.10
  13.8 9.2 %collective-permute-done.10.a = f32[256,128]{1,0:T(8,128)S(1)} collective-permute-done((f32[256,128]{1,0:T(8,128)S(1)}, f32[256,128]{1,0:T(8,128)S(1)}, u32[]{:S(2)}, u32[]{:S(2)}) %collective-permute-start.10) | collective-permute-done | bytes 131104 | tf_op jit(solution)/shard_map/ppermute | solution.py:425
  23.6 1.3 collective-permute-start.11
  24.9 1.9 %collective-permute-done.11.a = f32[256,128]{1,0:T(8,128)S(1)} collective-permute-done((f32[256,128]{1,0:T(8,128)S(1)}, f32[256,128]{1,0:T(8,128)S(1)}, u32[]{:S(2)}, u32[]{:S(2)}) %collective-permute-start.11) | collective-permute-done | bytes 131104 | tf_op jit(solution)/shard_map/ppermute | solution.py:425
  27.4 1.3 collective-permute-start.12
  28.8 8.4 %collective-permute-done.2.refs_2_ = f32[128,1024]{1,0:T(8,128)S(1)} collective-permute-done((f32[128,1024]{1,0:T(8,128)S(1)}, f32[128,1024]{1,0:T(8,128)S(1)}, u32[]{:S(2)}, u32[]{:S(2)}) %collective-permute-start.2) | collective-permute-done | bytes 524320 | tf_op jit(solution)/shard_map/ppermute | solution.py:410
  37.4 1.4 %collective-permute-start.7 = (f32[128,256]{1,0:T(8,128)S(1)}, f32[128,256]{1,0:T(8,128)S(1)}, u32[]{:S(2)}, u32[]{:S(2)}) collective-permute-start(f32[128,256]{1,0:T(8,128)S(1)} %get-tuple-element.65), channel_id=1, source_target_pairs={{0,64},{64,128},{128,192},{192,0},{1,65},{65,129},{129,193},{193,1... | collective-permute-start | bytes 393224 | tf_op jit(solution)/shard_map/ppermute | solution.py:410
  38.8 2.6 %collective-permute-start.8 = (f32[128,256]{1,0:T(8,128)S(1)}, f32[128,256]{1,0:T(8,128)S(1)}, u32[]{:S(2)}, u32[]{:S(2)}) collective-permute-start(f32[128,256]{1,0:T(8,128)S(1)} %get-tuple-element.66), channel_id=1, source_target_pairs={{0,128},{64,192},{128,0},{192,64},{1,129},{65,193},{129,1},{193,65... | collective-permute-start | bytes 393224 | tf_op jit(solution)/shard_map/ppermute | solution.py:410
  41.4 1.1 collective-permute-start.9
  43.4 3.9 %collective-permute-done.8.c = f32[128,256]{1,0:T(8,128)S(1)} collective-permute-done((f32[128,256]{1,0:T(8,128)S(1)}, f32[128,256]{1,0:T(8,128)S(1)}, u32[]{:S(2)}, u32[]{:S(2)}) %collective-permute-start.8) | collective-permute-done | bytes 131104 | tf_op jit(solution)/shard_map/ppermute | solution.py:410
  49.1 1.6 %collective-permute-done.15.refs_3_ = f32[128,128]{1,0:T(8,128)S(1)} collective-permute-done((f32[128,128]{1,0:T(8,128)S(1)}, f32[128,128]{1,0:T(8,128)S(1)}, u32[]{:S(2)}, u32[]{:S(2)}) %collective-permute-start.15) | collective-permute-done | bytes 65568 | tf_op jit(solution)/shard_map/ppermute | solution.py:410
  50.8 1.6 %collective-permute-done.14.refs_2_ = f32[128,128]{1,0:T(8,128)S(1)} collective-permute-done((f32[128,128]{1,0:T(8,128)S(1)}, f32[128,128]{1,0:T(8,128)S(1)}, u32[]{:S(2)}, u32[]{:S(2)}) %collective-permute-start.14) | collective-permute-done | bytes 65568 | tf_op jit(solution)/shard_map/ppermute | solution.py:410
  53.2 2.1 %collective-permute-start.18 = (f32[128,128]{1,0:T(8,128)S(1)}, f32[128,128]{1,0:T(8,128)S(1)}, u32[]{:S(2)}, u32[]{:S(2)}) collective-permute-start(f32[128,128]{1,0:T(8,128)S(1)} %total.9.refs_0_), channel_id=1, source_target_pairs={{0,192},{64,0},{128,64},{192,128},{1,193},{65,1},{129,65},{193,129... | collective-permute-start | bytes 196616 | tf_op jit(solution)/shard_map/ppermute | solution.py:410
  56.7 3.3 %collective-permute-done.17.refs_2_ = f32[128,128]{1,0:T(8,128)S(1)} collective-permute-done((f32[128,128]{1,0:T(8,128)S(1)}, f32[128,128]{1,0:T(8,128)S(1)}, u32[]{:S(2)}, u32[]{:S(2)}) %collective-permute-start.17) | collective-permute-done | bytes 65568 | tf_op jit(solution)/shard_map/ppermute | solution.py:410
  60.7 4.3 %collective-permute-start.19 = (f32[128,128]{1,0:T(8,128)S(1)}, f32[128,128]{1,0:T(8,128)S(1)}, u32[]{:S(2)}, u32[]{:S(2)}) collective-permute-start(f32[128,128]{1,0:T(8,128)S(1)} %total.10.refs_0_), channel_id=1, source_target_pairs={{0,8},{8,0},{1,9},{9,1},{2,10},{10,2},{3,11},{11,3},{4,12},{12,4},... | collective-permute-start | bytes 196616 | tf_op jit(solution)/shard_map/ppermute | solution.py:410
  66.2 17.4 %all_to_all.10.a = f32[8,48,128]{2,1,0:T(8,128)S(1)} all-to-all(f32[8,48,128]{2,1,0:T(8,128)S(1)} %products.1), channel_id=1, replica_groups=mesh['y'=4,'x'=4,'core'=2,'z'=8] {'z'}, dimensions={0} | all-to-all | bytes 393216 | tf_op jit(solution)/shard_map/all_to_all | solution.py:453
  83.7 11.3 %all_to_all.11.a = f32[8,48,128]{2,1,0:T(8,128)S(1)} all-to-all(f32[8,48,128]{2,1,0:T(8,128)S(1)} %sum_copies.1), channel_id=1, replica_groups=mesh['y'=4,'x'=4,'core'=2,'z'=8] {'z'}, dimensions={0} | all-to-all | bytes 393216 | tf_op jit(solution)/shard_map/all_to_all | solution.py:454
  96.8 2.1 %collective-permute-done.22.refs_3_ = f32[256,128]{1,0:T(8,128)S(1)} collective-permute-done((f32[256,128]{1,0:T(8,128)S(1)}, f32[256,128]{1,0:T(8,128)S(1)}, u32[]{:S(2)}, u32[]{:S(2)}) %collective-permute-start.22) | collective-permute-done | bytes 131104 | tf_op jit(solution)/shard_map/ppermute | solution.py:410
  98.9 1.7 %collective-permute-done.21.refs_2_ = f32[256,128]{1,0:T(8,128)S(1)} collective-permute-done((f32[256,128]{1,0:T(8,128)S(1)}, f32[256,128]{1,0:T(8,128)S(1)}, u32[]{:S(2)}, u32[]{:S(2)}) %collective-permute-start.21) | collective-permute-done | bytes 131104 | tf_op jit(solution)/shard_map/ppermute | solution.py:410
  100.6 1.3 collective-permute-done.20.refs_1_
  102.0 1.8 %collective-permute-start.25 = (f32[1024,128]{1,0:T(8,128)S(1)}, f32[1024,128]{1,0:T(8,128)S(1)}, u32[]{:S(2)}, u32[]{:S(2)}) collective-permute-start(f32[1024,128]{1,0:T(8,128)S(1)} %stack.22.refs_0_.refs_17_), channel_id=1, source_target_pairs={{0,48},{16,0},{32,16},{48,32},{1,49},{17,1},{33,17},{49,33},{2,50}... | collective-permute-start | bytes 1572872 | tf_op jit(solution)/shard_map/ppermute | solution.py:410
  103.8 4.6 %collective-permute-start.23 = (f32[1024,128]{1,0:T(8,128)S(1)}, f32[1024,128]{1,0:T(8,128)S(1)}, u32[]{:S(2)}, u32[]{:S(2)}) collective-permute-start(f32[1024,128]{1,0:T(8,128)S(1)} %stack.22.refs_0_.refs_17_), channel_id=1, source_target_pairs={{0,8},{8,0},{1,9},{9,1},{2,10},{10,2},{3,11},{11,3},{4,12},{12,4},... | collective-permute-start | bytes 1572872 | tf_op jit(solution)/shard_map/ppermute | solution.py:410
  108.4 7.0 %invert.1 = (f32[128,128]{1,0:T(8,128)S(1)}, bf16[384,256]{1,0:T(8,128)(2,1)S(1)}) custom-call(f32[128,128]{1,0:T(8,128)S(1)} %get-tuple-element.73.g_ref, f32[128,128]{1,0:T(8,128)S(1)} %total.11.p_ref), custom_call_target="tpu_custom_call" | custom-call | flops 8000000000 | bytes 262144 | tf_op jit(solution)/shard_map/invert/pallas_call | solution.py:312
  115.4 3.4 %finish.4 = (bf16[128,8192]{1,0:T(8,128)(2,1)}, f32[128,8192]{1,0:T(8,128)}, f32[128,8192]{1,0:T(8,128)}, bf16[128,8192]{1,0:T(8,128)(2,1)}) custom-call(s32[4]{0:T(128)S(1)} %pad_add_fusion.at, f32[1024,128]{1,0:T(8,128)S(1)} %stack.22.refs_0_.refs_17_, f32[1024,128]{1,0:T(8,128)S(1)} %collective-permute-done.23.refs_1_.refs_18_, ...), custom_call_target="tpu_custom_call" | custom-call | tf_op jit(solution)/shard_map/finish/pallas_call | solution.py:396
  120.1 2.7 %collective-permute-start.29 = (f32[512,128]{1,0:T(8,128)S(1)}, f32[512,128]{1,0:T(8,128)S(1)}, u32[]{:S(2)}, u32[]{:S(2)}) collective-permute-start(f32[512,128]{1,0:T(8,128)S(1)} %get-tuple-element.94), channel_id=1, source_target_pairs={{0,48},{16,0},{32,16},{48,32},{1,49},{17,1},{33,17},{49,33},{2,50}... | collective-permute-start | bytes 786440 | tf_op jit(solution)/shard_map/ppermute | solution.py:410
  122.8 3.4 %finish.5 = (bf16[128,8192]{1,0:T(8,128)(2,1)}, f32[128,8192]{1,0:T(8,128)}, f32[128,8192]{1,0:T(8,128)}, bf16[128,8192]{1,0:T(8,128)(2,1)}) custom-call(s32[4]{0:T(128)S(1)} %pad_add_fusion.at, f32[1024,128]{1,0:T(8,128)S(1)} %collective-permute-done.24.refs_0_.a_ref.refs_19_, ...), custom_call_target="tpu_custom_call", output_to_operand_aliasing={{0}: (14, {}), {1}: (15, {}), {2}: (16, {}), {3}: (17, {})} | custom-call | tf_op jit(solution)/shard_map/finish/pallas_call | solution.py:396
  126.1 3.4 %finish.6 = (bf16[128,8192]{1,0:T(8,128)(2,1)}, f32[128,8192]{1,0:T(8,128)}, f32[128,8192]{1,0:T(8,128)}, bf16[128,8192]{1,0:T(8,128)(2,1)}) custom-call(s32[4]{0:T(128)S(1)} %pad_add_fusion.at, f32[1024,128]{1,0:T(8,128)S(1)} %collective-permute-done.25.refs_0_.b_ref.refs_21_, ...), custom_call_target="tpu_custom_call", output_to_operand_aliasing={{0}: (14, {}), {1}: (15, {}), {2}: (16, {}), {3}: (17, {})} | custom-call | tf_op jit(solution)/shard_map/finish/pallas_call | solution.py:396
  130.1 1.5 %collective-permute-done.30.refs_1_ = f32[1024,128]{1,0:T(8,128)S(1)} collective-permute-done((f32[1024,128]{1,0:T(8,128)S(1)}, f32[1024,128]{1,0:T(8,128)S(1)}, u32[]{:S(2)}, u32[]{:S(2)}) %collective-permute-start.30) | collective-permute-done | bytes 524320 | tf_op jit(solution)/shard_map/ppermute | solution.py:410
  131.6 4.3 %finish.7 = (bf16[128,8192]{1,0:T(8,128)(2,1)}, f32[128,8192]{1,0:T(8,128)}, f32[128,8192]{1,0:T(8,128)}, bf16[128,8192]{1,0:T(8,128)(2,1)}, f32[1024,128]{1,0:T(8,128)}) custom-call(s32[4]{0:T(128)S(1)} %pad_add_fusion.at, f32[1024,128]{1,0:T(8,128)S(1)} %stack.23.refs_0_, ...), custom_call_target="tpu_custom_call", output_to_operand_aliasing={{0}: (14, {}), {1}: (15, {}), {2}: (16, {}), {3}: (17, {})} | custom-call | tf_op jit(solution)/shard_map/finish/pallas_call | solution.py:396
  (68 shorter events, 17.3 us)
Async XLA Ops:
  4.7 4.9 %collective-permute-start.5 = (f32[128,1024]{1,0:T(8,128)S(1)}, f32[128,1024]{1,0:T(8,128)S(1)}, u32[]{:S(2)}, u32[]{:S(2)}) collective-permute-start(f32[128,1024]{1,0:T(8,128)S(1)} %get-tuple-element.63.refs_9_), channel_id=1, source_target_pairs={{0,8},{8,0},{1,9},{9,1},{2,10},{10,2},{3,11},{11,3},{4,12},{12,4},... | collective-permute-start | bytes 1572872 | tf_op jit(solution)/shard_map/ppermute | solution.py:410
  8.1 2.4 %collective-permute-start.3 = (f32[128,1024]{1,0:T(8,128)S(1)}, f32[128,1024]{1,0:T(8,128)S(1)}, u32[]{:S(2)}, u32[]{:S(2)}) collective-permute-start(f32[128,1024]{1,0:T(8,128)S(1)} %get-tuple-element.61.refs_8_), channel_id=1, source_target_pairs={{0,8},{8,0},{1,9},{9,1},{2,10},{10,2},{3,11},{11,3},{4,12},{12,4},... | collective-permute-start | bytes 1572872 | tf_op jit(solution)/shard_map/ppermute | solution.py:410
  8.2 3.3 %collective-permute-start.1 = (f32[128,1024]{1,0:T(8,128)S(1)}, f32[128,1024]{1,0:T(8,128)S(1)}, u32[]{:S(2)}, u32[]{:S(2)}) collective-permute-start(f32[128,1024]{1,0:T(8,128)S(1)} %get-tuple-element.59.refs_7_), channel_id=1, source_target_pairs={{0,8},{8,0},{1,9},{9,1},{2,10},{10,2},{3,11},{11,3},{4,12},{12,4},... | collective-permute-start | bytes 1572872 | tf_op jit(solution)/shard_map/ppermute | solution.py:410
  8.6 20.2 %collective-permute-start = (f32[128,1024]{1,0:T(8,128)S(1)}, f32[128,1024]{1,0:T(8,128)S(1)}, u32[]{:S(2)}, u32[]{:S(2)}) collective-permute-start(f32[128,1024]{1,0:T(8,128)S(1)} %get-tuple-element.57.refs_6_), channel_id=1, source_target_pairs={{0,8},{8,0},{1,9},{9,1},{2,10},{10,2},{3,11},{11,3},{4,12},{12,4},... | collective-permute-start | bytes 1572872 | tf_op jit(solution)/shard_map/ppermute | solution.py:410
  9.7 19.1 %collective-permute-start.6 = (f32[128,1024]{1,0:T(8,128)S(1)}, f32[128,1024]{1,0:T(8,128)S(1)}, u32[]{:S(2)}, u32[]{:S(2)}) collective-permute-start(f32[128,1024]{1,0:T(8,128)S(1)} %total.8), channel_id=1, source_target_pairs={{0,48},{16,0},{32,16},{48,32},{1,49},{17,1},{33,17},{49,33},{2,50}... | collective-permute-start | bytes 1572872 | tf_op jit(solution)/shard_map/ppermute | solution.py:410
  10.5 18.2 %collective-permute-start.4 = (f32[128,1024]{1,0:T(8,128)S(1)}, f32[128,1024]{1,0:T(8,128)S(1)}, u32[]{:S(2)}, u32[]{:S(2)}) collective-permute-start(f32[128,1024]{1,0:T(8,128)S(1)} %total.7), channel_id=1, source_target_pairs={{0,32},{16,48},{32,0},{48,16},{1,33},{17,49},{33,1},{49,17},{2,34}... | collective-permute-start | bytes 1572872 | tf_op jit(solution)/shard_map/ppermute | solution.py:410
  11.6 25.6 %collective-permute-start.2 = (f32[128,1024]{1,0:T(8,128)S(1)}, f32[128,1024]{1,0:T(8,128)S(1)}, u32[]{:S(2)}, u32[]{:S(2)}) collective-permute-start(f32[128,1024]{1,0:T(8,128)S(1)} %total.6), channel_id=1, source_target_pairs={{0,16},{16,32},{32,48},{48,0},{1,17},{17,33},{33,49},{49,1},{2,18}... | collective-permute-start | bytes 1572872 | tf_op jit(solution)/shard_map/ppermute | solution.py:410
  12.5 10.5 %collective-permute-start.10 = (f32[256,128]{1,0:T(8,128)S(1)}, f32[256,128]{1,0:T(8,128)S(1)}, u32[]{:S(2)}, u32[]{:S(2)}) collective-permute-start(f32[256,128]{1,0:T(8,128)S(1)} %rows_of.1.b), channel_id=1, source_target_pairs={{0,4},{12,8},{17,21},{29,25},{34,38},{46,42},{51,55},{63,59},{64,6... | collective-permute-start | bytes 393224 | tf_op jit(solution)/shard_map/ppermute | solution.py:425
  23.6 3.2 %collective-permute-start.11 = (f32[256,128]{1,0:T(8,128)S(1)}, f32[256,128]{1,0:T(8,128)S(1)}, u32[]{:S(2)}, u32[]{:S(2)}) collective-permute-start(f32[256,128]{1,0:T(8,128)S(1)} %choose.3.b), channel_id=1, source_target_pairs={{0,2},{4,6},{12,14},{8,10},{17,19},{21,23},{29,31},{25,27},{34,36}... | collective-permute-start | bytes 393224 | tf_op jit(solution)/shard_map/ppermute | solution.py:425
  27.4 15.0 %collective-permute-start.12 = (f32[256,128]{1,0:T(8,128)S(1)}, f32[256,128]{1,0:T(8,128)S(1)}, u32[]{:S(2)}, u32[]{:S(2)}) collective-permute-start(f32[256,128]{1,0:T(8,128)S(1)} %choose.4.b), channel_id=1, source_target_pairs={{0,1},{4,5},{2,3},{6,7},{12,13},{8,9},{14,15},{10,11},{17,18},{21,... | collective-permute-start | bytes 393224 | tf_op jit(solution)/shard_map/ppermute | solution.py:425
  37.4 6.0 %collective-permute-start.7 = (f32[128,256]{1,0:T(8,128)S(1)}, f32[128,256]{1,0:T(8,128)S(1)}, u32[]{:S(2)}, u32[]{:S(2)}) collective-permute-start(f32[128,256]{1,0:T(8,128)S(1)} %get-tuple-element.65), channel_id=1, source_target_pairs={{0,64},{64,128},{128,192},{192,0},{1,65},{65,129},{129,193},{193,1... | collective-permute-start | bytes 393224 | tf_op jit(solution)/shard_map/ppermute | solution.py:410
  38.8 8.5 %collective-permute-start.8 = (f32[128,256]{1,0:T(8,128)S(1)}, f32[128,256]{1,0:T(8,128)S(1)}, u32[]{:S(2)}, u32[]{:S(2)}) collective-permute-start(f32[128,256]{1,0:T(8,128)S(1)} %get-tuple-element.66), channel_id=1, source_target_pairs={{0,128},{64,192},{128,0},{192,64},{1,129},{65,193},{129,1},{193,65... | collective-permute-start | bytes 393224 | tf_op jit(solution)/shard_map/ppermute | solution.py:410
  41.4 5.9 %collective-permute-start.9 = (f32[128,256]{1,0:T(8,128)S(1)}, f32[128,256]{1,0:T(8,128)S(1)}, u32[]{:S(2)}, u32[]{:S(2)}) collective-permute-start(f32[128,256]{1,0:T(8,128)S(1)} %get-tuple-element.67), channel_id=1, source_target_pairs={{0,192},{64,0},{128,64},{192,128},{1,193},{65,1},{129,65},{193,129... | collective-permute-start | bytes 393224 | tf_op jit(solution)/shard_map/ppermute | solution.py:410
  47.6 3.2 %collective-permute-start.15 = (f32[128,128]{1,0:T(8,128)S(1)}, f32[128,128]{1,0:T(8,128)S(1)}, u32[]{:S(2)}, u32[]{:S(2)}) collective-permute-start(f32[128,128]{1,0:T(8,128)S(1)} %get-tuple-element.69.refs_0_), channel_id=1, source_target_pairs={{0,48},{16,0},{32,16},{48,32},{1,49},{17,1},{33,17},{49,33},{2,50}... | collective-permute-start | bytes 196616 | tf_op jit(solution)/shard_map/ppermute | solution.py:410
  47.7 4.7 %collective-permute-start.14 = (f32[128,128]{1,0:T(8,128)S(1)}, f32[128,128]{1,0:T(8,128)S(1)}, u32[]{:S(2)}, u32[]{:S(2)}) collective-permute-start(f32[128,128]{1,0:T(8,128)S(1)} %get-tuple-element.69.refs_0_), channel_id=1, source_target_pairs={{0,32},{16,48},{32,0},{48,16},{1,33},{17,49},{33,1},{49,17},{2,34}... | collective-permute-start | bytes 196616 | tf_op jit(solution)/shard_map/ppermute | solution.py:410
  48.2 5.0 %collective-permute-start.13 = (f32[128,128]{1,0:T(8,128)S(1)}, f32[128,128]{1,0:T(8,128)S(1)}, u32[]{:S(2)}, u32[]{:S(2)}) collective-permute-start(f32[128,128]{1,0:T(8,128)S(1)} %get-tuple-element.69.refs_0_), channel_id=1, source_target_pairs={{0,16},{16,32},{32,48},{48,0},{1,17},{17,33},{33,49},{49,1},{2,18}... | collective-permute-start | bytes 196616 | tf_op jit(solution)/shard_map/ppermute | solution.py:410
  53.2 3.5 %collective-permute-start.18 = (f32[128,128]{1,0:T(8,128)S(1)}, f32[128,128]{1,0:T(8,128)S(1)}, u32[]{:S(2)}, u32[]{:S(2)}) collective-permute-start(f32[128,128]{1,0:T(8,128)S(1)} %total.9.refs_0_), channel_id=1, source_target_pairs={{0,192},{64,0},{128,64},{192,128},{1,193},{65,1},{129,65},{193,129... | collective-permute-start | bytes 196616 | tf_op jit(solution)/shard_map/ppermute | solution.py:410
  55.3 4.6 %collective-permute-start.17 = (f32[128,128]{1,0:T(8,128)S(1)}, f32[128,128]{1,0:T(8,128)S(1)}, u32[]{:S(2)}, u32[]{:S(2)}) collective-permute-start(f32[128,128]{1,0:T(8,128)S(1)} %total.9.refs_0_), channel_id=1, source_target_pairs={{0,128},{64,192},{128,0},{192,64},{1,129},{65,193},{129,1},{193,65... | collective-permute-start | bytes 196616 | tf_op jit(solution)/shard_map/ppermute | solution.py:410
  56.1 4.5 %collective-permute-start.16 = (f32[128,128]{1,0:T(8,128)S(1)}, f32[128,128]{1,0:T(8,128)S(1)}, u32[]{:S(2)}, u32[]{:S(2)}) collective-permute-start(f32[128,128]{1,0:T(8,128)S(1)} %total.9.refs_0_), channel_id=1, source_target_pairs={{0,64},{64,128},{128,192},{192,0},{1,65},{65,129},{129,193},{193,1... | collective-permute-start | bytes 196616 | tf_op jit(solution)/shard_map/ppermute | solution.py:410
  60.7 5.2 %collective-permute-start.19 = (f32[128,128]{1,0:T(8,128)S(1)}, f32[128,128]{1,0:T(8,128)S(1)}, u32[]{:S(2)}, u32[]{:S(2)}) collective-permute-start(f32[128,128]{1,0:T(8,128)S(1)} %total.10.refs_0_), channel_id=1, source_target_pairs={{0,8},{8,0},{1,9},{9,1},{2,10},{10,2},{3,11},{11,3},{4,12},{12,4},... | collective-permute-start | bytes 196616 | tf_op jit(solution)/shard_map/ppermute | solution.py:410
  95.0 3.9 %collective-permute-start.22 = (f32[256,128]{1,0:T(8,128)S(1)}, f32[256,128]{1,0:T(8,128)S(1)}, u32[]{:S(2)}, u32[]{:S(2)}) collective-permute-start(f32[256,128]{1,0:T(8,128)S(1)} %get-tuple-element.70.refs_0_), channel_id=1, source_target_pairs={{0,192},{64,0},{128,64},{192,128},{1,193},{65,1},{129,65},{193,129... | collective-permute-start | bytes 393224 | tf_op jit(solution)/shard_map/ppermute | solution.py:410
  95.2 5.4 %collective-permute-start.21 = (f32[256,128]{1,0:T(8,128)S(1)}, f32[256,128]{1,0:T(8,128)S(1)}, u32[]{:S(2)}, u32[]{:S(2)}) collective-permute-start(f32[256,128]{1,0:T(8,128)S(1)} %get-tuple-element.70.refs_0_), channel_id=1, source_target_pairs={{0,128},{64,192},{128,0},{192,64},{1,129},{65,193},{129,1},{193,65... | collective-permute-start | bytes 393224 | tf_op jit(solution)/shard_map/ppermute | solution.py:410
  96.2 5.7 %collective-permute-start.20 = (f32[256,128]{1,0:T(8,128)S(1)}, f32[256,128]{1,0:T(8,128)S(1)}, u32[]{:S(2)}, u32[]{:S(2)}) collective-permute-start(f32[256,128]{1,0:T(8,128)S(1)} %get-tuple-element.70.refs_0_), channel_id=1, source_target_pairs={{0,64},{64,128},{128,192},{192,0},{1,65},{65,129},{129,193},{193,1... | collective-permute-start | bytes 393224 | tf_op jit(solution)/shard_map/ppermute | solution.py:410
  102.0 13.4 %copy-start = (f32[128,8192]{1,0:T(8,128)S(1)}, f32[128,8192]{1,0:T(8,128)}, u32[]{:S(2)}) copy-start(f32[128,8192]{1,0:T(8,128)} %refs_11_.7) | copy-start | bytes 12582916
  102.0 16.8 %collective-permute-start.25 = (f32[1024,128]{1,0:T(8,128)S(1)}, f32[1024,128]{1,0:T(8,128)S(1)}, u32[]{:S(2)}, u32[]{:S(2)}) collective-permute-start(f32[1024,128]{1,0:T(8,128)S(1)} %stack.22.refs_0_.refs_17_), channel_id=1, source_target_pairs={{0,48},{16,0},{32,16},{48,32},{1,49},{17,1},{33,17},{49,33},{2,50}... | collective-permute-start | bytes 1572872 | tf_op jit(solution)/shard_map/ppermute | solution.py:410
  103.8 15.0 %collective-permute-start.24 = (f32[1024,128]{1,0:T(8,128)S(1)}, f32[1024,128]{1,0:T(8,128)S(1)}, u32[]{:S(2)}, u32[]{:S(2)}) collective-permute-start(f32[1024,128]{1,0:T(8,128)S(1)} %stack.22.refs_0_.refs_17_), channel_id=1, source_target_pairs={{0,16},{16,32},{32,48},{48,0},{1,17},{17,33},{33,49},{49,1},{2,18}... | collective-permute-start | bytes 1572872 | tf_op jit(solution)/shard_map/ppermute | solution.py:410
  103.8 11.6 %collective-permute-start.23 = (f32[1024,128]{1,0:T(8,128)S(1)}, f32[1024,128]{1,0:T(8,128)S(1)}, u32[]{:S(2)}, u32[]{:S(2)}) collective-permute-start(f32[1024,128]{1,0:T(8,128)S(1)} %stack.22.refs_0_.refs_17_), channel_id=1, source_target_pairs={{0,8},{8,0},{1,9},{9,1},{2,10},{10,2},{3,11},{11,3},{4,12},{12,4},... | collective-permute-start | bytes 1572872 | tf_op jit(solution)/shard_map/ppermute | solution.py:410
  118.8 4.0 %collective-permute-start.27 = (f32[1024,128]{1,0:T(8,128)S(1)}, f32[1024,128]{1,0:T(8,128)S(1)}, u32[]{:S(2)}, u32[]{:S(2)}) collective-permute-start(f32[1024,128]{1,0:T(8,128)S(1)} %collective-permute-done.24.refs_0_.a_ref.refs_19_), channel_id=1, source_target_pairs={{0,8},{8,0},{1,9},{9,1},{2,10},{10,2},{3,11},{11,3},{4,12},{12,4},... | collective-permute-start | bytes 1572872 | tf_op jit(solution)/shard_map/ppermute | solution.py:410
  119.4 6.8 %collective-permute-start.26 = (f32[1024,128]{1,0:T(8,128)S(1)}, f32[1024,128]{1,0:T(8,128)S(1)}, u32[]{:S(2)}, u32[]{:S(2)}) collective-permute-start(f32[1024,128]{1,0:T(8,128)S(1)} %collective-permute-done.25.refs_0_.b_ref.refs_21_), channel_id=1, source_target_pairs={{0,8},{8,0},{1,9},{9,1},{2,10},{10,2},{3,11},{11,3},{4,12},{12,4},... | collective-permute-start | bytes 1572872 | tf_op jit(solution)/shard_map/ppermute | solution.py:410
  119.4 10.1 %collective-permute-start.28 = (f32[512,128]{1,0:T(8,128)S(1)}, f32[512,128]{1,0:T(8,128)S(1)}, u32[]{:S(2)}, u32[]{:S(2)}) collective-permute-start(f32[512,128]{1,0:T(8,128)S(1)} %get-tuple-element.93), channel_id=1, source_target_pairs={{0,16},{16,32},{32,48},{48,0},{1,17},{17,33},{33,49},{49,1},{2,18}... | collective-permute-start | bytes 786440 | tf_op jit(solution)/shard_map/ppermute | solution.py:410
  120.1 9.4 %collective-permute-start.29 = (f32[512,128]{1,0:T(8,128)S(1)}, f32[512,128]{1,0:T(8,128)S(1)}, u32[]{:S(2)}, u32[]{:S(2)}) collective-permute-start(f32[512,128]{1,0:T(8,128)S(1)} %get-tuple-element.94), channel_id=1, source_target_pairs={{0,48},{16,0},{32,16},{48,32},{1,49},{17,1},{33,17},{49,33},{2,50}... | collective-permute-start | bytes 786440 | tf_op jit(solution)/shard_map/ppermute | solution.py:410
  129.5 2.1 %collective-permute-start.30 = (f32[1024,128]{1,0:T(8,128)S(1)}, f32[1024,128]{1,0:T(8,128)S(1)}, u32[]{:S(2)}, u32[]{:S(2)}) collective-permute-start(f32[1024,128]{1,0:T(8,128)S(1)} %stack.23.refs_0_), channel_id=1, source_target_pairs={{0,8},{8,0},{1,9},{9,1},{2,10},{10,2},{3,11},{11,3},{4,12},{12,4},... | collective-permute-start | bytes 1572872 | tf_op jit(solution)/shard_map/ppermute | solution.py:410
  (4 other events, 20.0 us)
where the time goes:
time: 136 us
  waiting for transfers between devices  40.1 us (29%)
  starting transfers between devices  36.5 us (27%)
  blocking collectives  28.7 us (21%)
  Pallas kernels  26.4 us (19%)
  local copies, waits for them, and re-layouts  3.2 us (2%)
    ppermute x28, starting transfers between devices, shift(): return lax.ppermute(value, axis, [(i, (i + step) % n) for i in range(n)])  32.6 us
    ppermute x28, waiting for transfers between devices, shift(): return lax.ppermute(value, axis, [(i, (i + step) % n) for i in range(n)])  28.9 us
    all_to_all x1, blocking collectives, on_device(): whole = lax.all_to_all(products(m, p), 'z', 0, 0)  17.4 us
    pallas_call x4, Pallas kernels, finish(): pl.pallas_call(body, grid_spec=pltpu.PrefetchScalarGridSpec(num_scalar_pr...  14.4 us
    all_to_all x1, blocking collectives, on_device(): whole = lax.all_to_all(sum_copies(whole), 'z', 0, 0)  11.3 us
    ppermute x3, waiting for transfers between devices, spread(): return lax.ppermute(block, ALL, pairs)  11.2 us
    pallas_call x1, Pallas kernels, invert(): pl.pallas_call(body, in_specs=[vmem()] * 2, out_specs=[vmem()] * 2, out_s...  7 us
    ppermute x3, starting transfers between devices, spread(): return lax.ppermute(block, ALL, pairs)  3.89 us
  transfers between devices with their start and end apart: 31, of which 17 were waited for; matrix products, arithmetic and copies ran while one was open for 0% of the time, Pallas kernels for 15%

commit v1 on v0

--- a/solution.py
+++ b/solution.py
@@ -61,6 +61,44 @@
     )(place, grads, errors)
 
 
+def add_two(own, came):
+    rows, wide = own.shape
+    tall = rows // 2
+
+    def body(a, b, up, down):
+        up[...] = a[:tall] + b[:tall]
+        down[...] = a[tall:] + b[tall:]
+
+    return pl.pallas_call(
+        body,
+        in_specs=[vmem()] * 2,
+        out_specs=[vmem()] * 2,
+        out_shape=[jax.ShapeDtypeStruct((tall, wide), F32)] * 2,
+        compiler_params=params(),
+        name="add_two",
+    )(own, came)
+
+
+def add_half(own, came, part, side):
+    rows, wide = own.shape
+    tall = rows // 2
+
+    def body(a, b, c, out):
+        for i in range(2):
+            half = slice(i * tall, (i + 1) * tall)
+            value = a[half] + b[half]
+            out[half, :] = value + c[...] if i == side else value
+
+    return pl.pallas_call(
+        body,
+        in_specs=[vmem()] * 3,
+        out_specs=vmem(),
+        out_shape=jax.ShapeDtypeStruct((rows, wide), F32),
+        compiler_params=params(),
+        name="add_half",
+    )(own, came, part)
+
+
 def sum_split(parts):
     rows, wide = parts[0].shape
     thin = wide // 4
@@ -228,20 +266,23 @@
     )(place, q_prev)
 
 
-def choose(place, hits, came, have):
-    def body(at, a, b, out):
+def choose(place, hits, came, have, *after):
+    def body(at, a, b, *refs):
+        out = refs[-1]
         away = (at[3] + 8 - (at[0] * 4 + at[1])) % 8
         hit = functools.reduce(jnp.logical_or, [away == h for h in hits])
         out[...] = jnp.where(hit, a[...], b[...])
 
     return pl.pallas_call(
         body,
-        in_specs=[pl.BlockSpec(memory_space=pltpu.SMEM)] + [vmem()] * 2,
+        in_specs=[pl.BlockSpec(memory_space=pltpu.SMEM)]
+        + [vmem()] * 2
+        + [pl.BlockSpec(memory_space=pl.ANY)] * len(after),
         out_specs=vmem(),
         out_shape=jax.ShapeDtypeStruct(came.shape, F32),
         compiler_params=params(),
         name="choose",
-    )(place, came, have)
+    )(place, came, have, *after)
 
 
 ORDER = (0, 1, 3, 2)
@@ -431,19 +472,23 @@
     grads, errors = grads[0], errors[0]
 
     theirs = merge_half(place, True, grads, errors)
-    came = {k: shift(theirs[k], "core", 1) for k in (1, 2, 3, 0)}
+    came = {k: shift(theirs[k], "core", 1) for k in (2, 1, 3, 0)}
     mine = merge_half(place, False, grads, errors)
     merged = [*mine, *theirs]
 
     right = rows_of(place, q_prev)
-    held = [0]
-    for step in (4, 2, 1):
-        new = [h + step for h in held]
-        right = choose(place, new, spread(right, step, held), right)
-        held = held + new
-
-    parts = [shift(total([mine[k], came[k]]), "x", k) for k in (1, 2, 3)]
+    right = choose(place, [4], spread(right, 4, [0]), right)
+    second_step = spread(right, 2, [0, 4])
+
+    upper, lower = add_two(mine[2], came[2])
+    upper, lower = shift(upper, "x", 1), shift(lower, "x", 3)
+    parts = [
+        shift(add_half(mine[1], came[1], upper, 0), "x", 1),
+        shift(add_half(mine[3], came[3], lower, 1), "x", 3),
+    ]
     blocks = sum_split([mine[0], came[0], *parts])
+    right = choose(place, [2, 6], second_step, right, blocks[0])
+    right = choose(place, [1, 3, 5, 7], spread(right, 1, [0, 2, 4, 6]), right)
     m, p = left_part([blocks[0]] + [shift(blocks[k], "y", k) for k in (1, 2, 3)], right)
 
     for axis in ("x", "y"):

time: 136 us -> 138 us (1.015)
  starting transfers between devices: 36.5 us -> 48.6 us
  waiting for transfers between devices: 40.1 us -> 33.7 us
  blocking collectives: 28.7 us -> 24.5 us
    ppermute x28 -> x29, starting transfers between devices: 32.6 us -> 42.7 us  [shift(): return lax.ppermute(value, axis, [(i, (i + step) % n) for i in range(n)])]
    ppermute x28 -> x29, waiting for transfers between devices: 28.9 us -> 24.2 us  [shift(): return lax.ppermute(value, axis, [(i, (i + step) % n) for i in range(n)])]
    all_to_all x1, blocking collectives: 17.4 us -> 13.2 us  [on_device(): whole = lax.all_to_all(products(m, p), 'z', 0, 0)]
    ppermute x3, starting transfers between devices: 3.89 us -> 5.89 us  [spread(): return lax.ppermute(block, ALL, pairs)]
    ppermute x3, waiting for transfers between devices: 11.2 us -> 9.5 us  [spread(): return lax.ppermute(block, ALL, pairs)]
  transfers between devices with their start and end apart: 31 -> 32, of which waited for: 17 -> 18; matrix products, arithmetic and copies ran while one was open for 0% -> 0% of each run, Pallas kernels for 15% -> 15%
where the time goes in v1:
time: 138 us
  starting transfers between devices  48.6 us (35%)
  waiting for transfers between devices  33.7 us (24%)
  Pallas kernels  26.4 us (19%)
  blocking collectives  24.5 us (18%)
  local copies, waits for them, and re-layouts  3.2 us (2%)
    ppermute x29, starting transfers between devices, shift(): return lax.ppermute(value, axis, [(i, (i + step) % n) for i in range(n)])  42.7 us
    ppermute x29, waiting for transfers between devices, shift(): return lax.ppermute(value, axis, [(i, (i + step) % n) for i in range(n)])  24.2 us
    pallas_call x4, Pallas kernels, finish(): pl.pallas_call(body, grid_spec=pltpu.PrefetchScalarGridSpec(num_scalar_pr...  14.4 us
    all_to_all x1, blocking collectives, on_device(): whole = lax.all_to_all(products(m, p), 'z', 0, 0)  13.2 us
    all_to_all x1, blocking collectives, on_device(): whole = lax.all_to_all(sum_copies(whole), 'z', 0, 0)  11.3 us
    ppermute x3, waiting for transfers between devices, spread(): return lax.ppermute(block, ALL, pairs)  9.5 us
    pallas_call x1, Pallas kernels, invert(): pl.pallas_call(body, in_specs=[vmem()] * 2, out_specs=[vmem()] * 2, out_s...  7 us
    ppermute x3, starting transfers between devices, spread(): return lax.ppermute(block, ALL, pairs)  5.89 us
  transfers between devices with their start and end apart: 32, of which 18 were waited for; matrix products, arithmetic and copies ran while one was open for 0% of the time, Pallas kernels for 15%

profile of v1, /device:TPU:1, one launch (start us, length us, event | category | flops | bytes accessed | tf_op | source)
XLA Modules:
  0.0 137.5 jit_solution(2719574930597562365)
XLA Ops:
  0.7 1.6 %copy-done.2 = bf16[1,128,8192]{2,1,0:T(8,128)(2,1)S(1)} copy-done((bf16[1,128,8192]{2,1,0:T(8,128)(2,1)S(1)}, bf16[1,128,8192]{2,1,0:T(8,128)(2,1)}, u32[]{:S(2)}) %copy-start.2) | copy-done | bytes 2097176
  2.3 1.6 %copy-done.3 = bf16[1,128,8192]{2,1,0:T(8,128)(2,1)S(1)} copy-done((bf16[1,128,8192]{2,1,0:T(8,128)(2,1)S(1)}, bf16[1,128,8192]{2,1,0:T(8,128)(2,1)}, u32[]{:S(2)}) %copy-start.3) | copy-done | bytes 2097176
  4.7 3.3 %collective-permute-start.2 = (f32[128,1024]{1,0:T(8,128)S(1)}, f32[128,1024]{1,0:T(8,128)S(1)}, u32[]{:S(2)}, u32[]{:S(2)}) collective-permute-start(f32[128,1024]{1,0:T(8,128)S(1)} %get-tuple-element.63.refs_8_), channel_id=1, source_target_pairs={{0,8},{8,0},{1,9},{9,1},{2,10},{10,2},{3,11},{11,3},{4,12},{12,4},... | collective-permute-start | bytes 1572872 | tf_op jit(solution)/shard_map/ppermute | solution.py:451
  12.1 5.1 %collective-permute-done.6.c = f32[64,1024]{1,0:T(8,128)S(1)} collective-permute-done((f32[64,1024]{1,0:T(8,128)S(1)}, f32[64,1024]{1,0:T(8,128)S(1)}, u32[]{:S(2)}, u32[]{:S(2)}) %collective-permute-start.6) | collective-permute-done | bytes 262176 | tf_op jit(solution)/shard_map/ppermute | solution.py:451
  17.3 2.0 %collective-permute-start.7 = (f32[128,1024]{1,0:T(8,128)S(1)}, f32[128,1024]{1,0:T(8,128)S(1)}, u32[]{:S(2)}, u32[]{:S(2)}) collective-permute-start(f32[128,1024]{1,0:T(8,128)S(1)} %add_half.3), channel_id=1, source_target_pairs={{0,48},{16,0},{32,16},{48,32},{1,49},{17,1},{33,17},{49,33},{2,50}... | collective-permute-start | bytes 1572872 | tf_op jit(solution)/shard_map/ppermute | solution.py:451
  20.1 1.3 collective-permute-start.11
  21.4 9.2 %collective-permute-done.11.a = f32[256,128]{1,0:T(8,128)S(1)} collective-permute-done((f32[256,128]{1,0:T(8,128)S(1)}, f32[256,128]{1,0:T(8,128)S(1)}, u32[]{:S(2)}, u32[]{:S(2)}) %collective-permute-start.11) | collective-permute-done | bytes 131104 | tf_op jit(solution)/shard_map/ppermute | solution.py:466
  31.2 1.3 collective-permute-start.12
  32.8 1.4 collective-permute-start.8
  35.0 3.3 %collective-permute-start.13 = (f32[256,128]{1,0:T(8,128)S(1)}, f32[256,128]{1,0:T(8,128)S(1)}, u32[]{:S(2)}, u32[]{:S(2)}) collective-permute-start(f32[256,128]{1,0:T(8,128)S(1)} %choose.4.b), channel_id=1, source_target_pairs={{0,1},{2,3},{4,5},{6,7},{12,13},{14,15},{8,9},{10,11},{17,18},{19,... | collective-permute-start | bytes 393224 | tf_op jit(solution)/shard_map/ppermute | solution.py:466
  38.3 2.7 %collective-permute-start.9 = (f32[128,256]{1,0:T(8,128)S(1)}, f32[128,256]{1,0:T(8,128)S(1)}, u32[]{:S(2)}, u32[]{:S(2)}) collective-permute-start(f32[128,256]{1,0:T(8,128)S(1)} %get-tuple-element.70), channel_id=1, source_target_pairs={{0,128},{64,192},{128,0},{192,64},{1,129},{65,193},{129,1},{193,65... | collective-permute-start | bytes 393224 | tf_op jit(solution)/shard_map/ppermute | solution.py:451
  41.0 1.1 collective-permute-start.10
  42.7 1.1 collective-permute-done.9.c
  43.7 1.2 collective-permute-done.10.d
  46.7 1.9 %collective-permute-done.16.refs_3_ = f32[128,128]{1,0:T(8,128)S(1)} collective-permute-done((f32[128,128]{1,0:T(8,128)S(1)}, f32[128,128]{1,0:T(8,128)S(1)}, u32[]{:S(2)}, u32[]{:S(2)}) %collective-permute-start.16) | collective-permute-done | bytes 65568 | tf_op jit(solution)/shard_map/ppermute | solution.py:451
  48.7 1.5 %collective-permute-done.15.refs_2_ = f32[128,128]{1,0:T(8,128)S(1)} collective-permute-done((f32[128,128]{1,0:T(8,128)S(1)}, f32[128,128]{1,0:T(8,128)S(1)}, u32[]{:S(2)}, u32[]{:S(2)}) %collective-permute-start.15) | collective-permute-done | bytes 65568 | tf_op jit(solution)/shard_map/ppermute | solution.py:451
  50.9 2.2 %collective-permute-start.19 = (f32[128,128]{1,0:T(8,128)S(1)}, f32[128,128]{1,0:T(8,128)S(1)}, u32[]{:S(2)}, u32[]{:S(2)}) collective-permute-start(f32[128,128]{1,0:T(8,128)S(1)} %total.3.refs_0_), channel_id=1, source_target_pairs={{0,192},{64,0},{128,64},{192,128},{1,193},{65,1},{129,65},{193,129... | collective-permute-start | bytes 196616 | tf_op jit(solution)/shard_map/ppermute | solution.py:451
  54.4 3.3 %collective-permute-done.18.refs_2_ = f32[128,128]{1,0:T(8,128)S(1)} collective-permute-done((f32[128,128]{1,0:T(8,128)S(1)}, f32[128,128]{1,0:T(8,128)S(1)}, u32[]{:S(2)}, u32[]{:S(2)}) %collective-permute-start.18) | collective-permute-done | bytes 65568 | tf_op jit(solution)/shard_map/ppermute | solution.py:451
  58.7 12.5 %collective-permute-start.20 = (f32[128,128]{1,0:T(8,128)S(1)}, f32[128,128]{1,0:T(8,128)S(1)}, u32[]{:S(2)}, u32[]{:S(2)}) collective-permute-start(f32[128,128]{1,0:T(8,128)S(1)} %total.4.refs_0_), channel_id=1, source_target_pairs={{0,8},{8,0},{1,9},{9,1},{2,10},{10,2},{3,11},{11,3},{4,12},{12,4},... | collective-permute-start | bytes 196616 | tf_op jit(solution)/shard_map/ppermute | solution.py:451
  72.5 13.2 %all_to_all.10.a = f32[8,48,128]{2,1,0:T(8,128)S(1)} all-to-all(f32[8,48,128]{2,1,0:T(8,128)S(1)} %products.1), channel_id=1, replica_groups=mesh['y'=4,'x'=4,'core'=2,'z'=8] {'z'}, dimensions={0} | all-to-all | bytes 393216 | tf_op jit(solution)/shard_map/all_to_all | solution.py:498
  85.7 11.3 %all_to_all.11.a = f32[8,48,128]{2,1,0:T(8,128)S(1)} all-to-all(f32[8,48,128]{2,1,0:T(8,128)S(1)} %sum_copies.1), channel_id=1, replica_groups=mesh['y'=4,'x'=4,'core'=2,'z'=8] {'z'}, dimensions={0} | all-to-all | bytes 393216 | tf_op jit(solution)/shard_map/all_to_all | solution.py:499
  98.7 2.2 %collective-permute-done.23.refs_3_ = f32[256,128]{1,0:T(8,128)S(1)} collective-permute-done((f32[256,128]{1,0:T(8,128)S(1)}, f32[256,128]{1,0:T(8,128)S(1)}, u32[]{:S(2)}, u32[]{:S(2)}) %collective-permute-start.23) | collective-permute-done | bytes 131104 | tf_op jit(solution)/shard_map/ppermute | solution.py:451
  101.0 1.7 %collective-permute-done.22.refs_2_ = f32[256,128]{1,0:T(8,128)S(1)} collective-permute-done((f32[256,128]{1,0:T(8,128)S(1)}, f32[256,128]{1,0:T(8,128)S(1)}, u32[]{:S(2)}, u32[]{:S(2)}) %collective-permute-start.22) | collective-permute-done | bytes 131104 | tf_op jit(solution)/shard_map/ppermute | solution.py:451
  102.6 1.3 collective-permute-done.21.refs_1_
  105.6 4.6 %collective-permute-start.24 = (f32[1024,128]{1,0:T(8,128)S(1)}, f32[1024,128]{1,0:T(8,128)S(1)}, u32[]{:S(2)}, u32[]{:S(2)}) collective-permute-start(f32[1024,128]{1,0:T(8,128)S(1)} %stack.22.refs_0_.refs_17_), channel_id=1, source_target_pairs={{0,8},{8,0},{1,9},{9,1},{2,10},{10,2},{3,11},{11,3},{4,12},{12,4},... | collective-permute-start | bytes 1572872 | tf_op jit(solution)/shard_map/ppermute | solution.py:451
  110.2 7.0 %invert.1 = (f32[128,128]{1,0:T(8,128)S(1)}, bf16[384,256]{1,0:T(8,128)(2,1)S(1)}) custom-call(f32[128,128]{1,0:T(8,128)S(1)} %get-tuple-element.77.g_ref, f32[128,128]{1,0:T(8,128)S(1)} %total.5.p_ref), custom_call_target="tpu_custom_call" | custom-call | flops 8000000000 | bytes 262144 | tf_op jit(solution)/shard_map/invert/pallas_call | solution.py:353
  117.2 3.4 %finish.4 = (bf16[128,8192]{1,0:T(8,128)(2,1)}, f32[128,8192]{1,0:T(8,128)}, f32[128,8192]{1,0:T(8,128)}, bf16[128,8192]{1,0:T(8,128)(2,1)}) custom-call(s32[4]{0:T(128)S(1)} %pad_add_fusion.at, f32[1024,128]{1,0:T(8,128)S(1)} %stack.22.refs_0_.refs_17_, f32[1024,128]{1,0:T(8,128)S(1)} %collective-permute-done.24.refs_1_.refs_18_, ...), custom_call_target="tpu_custom_call" | custom-call | tf_op jit(solution)/shard_map/finish/pallas_call | solution.py:437
  121.3 2.7 %collective-permute-start.30 = (f32[512,128]{1,0:T(8,128)S(1)}, f32[512,128]{1,0:T(8,128)S(1)}, u32[]{:S(2)}, u32[]{:S(2)}) collective-permute-start(f32[512,128]{1,0:T(8,128)S(1)} %get-tuple-element.98), channel_id=1, source_target_pairs={{0,48},{16,0},{32,16},{48,32},{1,49},{17,1},{33,17},{49,33},{2,50}... | collective-permute-start | bytes 786440 | tf_op jit(solution)/shard_map/ppermute | solution.py:451
  124.0 3.3 %finish.5 = (bf16[128,8192]{1,0:T(8,128)(2,1)}, f32[128,8192]{1,0:T(8,128)}, f32[128,8192]{1,0:T(8,128)}, bf16[128,8192]{1,0:T(8,128)(2,1)}) custom-call(s32[4]{0:T(128)S(1)} %pad_add_fusion.at, f32[1024,128]{1,0:T(8,128)S(1)} %collective-permute-done.25.refs_0_.a_ref.refs_19_, ...), custom_call_target="tpu_custom_call", output_to_operand_aliasing={{0}: (14, {}), {1}: (15, {}), {2}: (16, {}), {3}: (17, {})} | custom-call | tf_op jit(solution)/shard_map/finish/pallas_call | solution.py:437
  127.4 3.4 %finish.6 = (bf16[128,8192]{1,0:T(8,128)(2,1)}, f32[128,8192]{1,0:T(8,128)}, f32[128,8192]{1,0:T(8,128)}, bf16[128,8192]{1,0:T(8,128)(2,1)}) custom-call(s32[4]{0:T(128)S(1)} %pad_add_fusion.at, f32[1024,128]{1,0:T(8,128)S(1)} %collective-permute-done.26.refs_0_.b_ref.refs_21_, ...), custom_call_target="tpu_custom_call", output_to_operand_aliasing={{0}: (14, {}), {1}: (15, {}), {2}: (16, {}), {3}: (17, {})} | custom-call | tf_op jit(solution)/shard_map/finish/pallas_call | solution.py:437
  131.5 1.5 %collective-permute-done.31.refs_1_ = f32[1024,128]{1,0:T(8,128)S(1)} collective-permute-done((f32[1024,128]{1,0:T(8,128)S(1)}, f32[1024,128]{1,0:T(8,128)S(1)}, u32[]{:S(2)}, u32[]{:S(2)}) %collective-permute-start.31) | collective-permute-done | bytes 524320 | tf_op jit(solution)/shard_map/ppermute | solution.py:451
  133.0 4.3 %finish.7 = (bf16[128,8192]{1,0:T(8,128)(2,1)}, f32[128,8192]{1,0:T(8,128)}, f32[128,8192]{1,0:T(8,128)}, bf16[128,8192]{1,0:T(8,128)(2,1)}, f32[1024,128]{1,0:T(8,128)}) custom-call(s32[4]{0:T(128)S(1)} %pad_add_fusion.at, f32[1024,128]{1,0:T(8,128)S(1)} %stack.23.refs_0_, ...), custom_call_target="tpu_custom_call", output_to_operand_aliasing={{0}: (14, {}), {1}: (15, {}), {2}: (16, {}), {3}: (17, {})} | custom-call | tf_op jit(solution)/shard_map/finish/pallas_call | solution.py:437
  (70 shorter events, 18.8 us)
Async XLA Ops:
  4.7 4.9 %collective-permute-start.2 = (f32[128,1024]{1,0:T(8,128)S(1)}, f32[128,1024]{1,0:T(8,128)S(1)}, u32[]{:S(2)}, u32[]{:S(2)}) collective-permute-start(f32[128,1024]{1,0:T(8,128)S(1)} %get-tuple-element.63.refs_8_), channel_id=1, source_target_pairs={{0,8},{8,0},{1,9},{9,1},{2,10},{10,2},{3,11},{11,3},{4,12},{12,4},... | collective-permute-start | bytes 1572872 | tf_op jit(solution)/shard_map/ppermute | solution.py:451
  8.1 4.1 %collective-permute-start.5 = (f32[128,1024]{1,0:T(8,128)S(1)}, f32[128,1024]{1,0:T(8,128)S(1)}, u32[]{:S(2)}, u32[]{:S(2)}) collective-permute-start(f32[128,1024]{1,0:T(8,128)S(1)} %get-tuple-element.66.refs_9_), channel_id=1, source_target_pairs={{0,8},{8,0},{1,9},{9,1},{2,10},{10,2},{3,11},{11,3},{4,12},{12,4},... | collective-permute-start | bytes 1572872 | tf_op jit(solution)/shard_map/ppermute | solution.py:451
  8.2 11.2 %collective-permute-start.1 = (f32[128,1024]{1,0:T(8,128)S(1)}, f32[128,1024]{1,0:T(8,128)S(1)}, u32[]{:S(2)}, u32[]{:S(2)}) collective-permute-start(f32[128,1024]{1,0:T(8,128)S(1)} %get-tuple-element.61.refs_7_), channel_id=1, source_target_pairs={{0,8},{8,0},{1,9},{9,1},{2,10},{10,2},{3,11},{11,3},{4,12},{12,4},... | collective-permute-start | bytes 1572872 | tf_op jit(solution)/shard_map/ppermute | solution.py:451
  9.7 7.6 %collective-permute-start.6 = (f32[64,1024]{1,0:T(8,128)S(1)}, f32[64,1024]{1,0:T(8,128)S(1)}, u32[]{:S(2)}, u32[]{:S(2)}) collective-permute-start(f32[64,1024]{1,0:T(8,128)S(1)} %get-tuple-element.67), channel_id=1, source_target_pairs={{0,48},{16,0},{32,16},{48,32},{1,49},{17,1},{33,17},{49,33},{2,50}... | collective-permute-start | bytes 786440 | tf_op jit(solution)/shard_map/ppermute | solution.py:451
  10.5 8.9 %collective-permute-start.3 = (f32[64,1024]{1,0:T(8,128)S(1)}, f32[64,1024]{1,0:T(8,128)S(1)}, u32[]{:S(2)}, u32[]{:S(2)}) collective-permute-start(f32[64,1024]{1,0:T(8,128)S(1)} %get-tuple-element.64), channel_id=1, source_target_pairs={{0,16},{16,32},{32,48},{48,0},{1,17},{17,33},{33,49},{49,1},{2,18}... | collective-permute-start | bytes 786440 | tf_op jit(solution)/shard_map/ppermute | solution.py:451
  11.2 21.3 %collective-permute-start = (f32[128,1024]{1,0:T(8,128)S(1)}, f32[128,1024]{1,0:T(8,128)S(1)}, u32[]{:S(2)}, u32[]{:S(2)}) collective-permute-start(f32[128,1024]{1,0:T(8,128)S(1)} %get-tuple-element.59.refs_6_), channel_id=1, source_target_pairs={{0,8},{8,0},{1,9},{9,1},{2,10},{10,2},{3,11},{11,3},{4,12},{12,4},... | collective-permute-start | bytes 1572872 | tf_op jit(solution)/shard_map/ppermute | solution.py:451
  17.3 15.2 %collective-permute-start.7 = (f32[128,1024]{1,0:T(8,128)S(1)}, f32[128,1024]{1,0:T(8,128)S(1)}, u32[]{:S(2)}, u32[]{:S(2)}) collective-permute-start(f32[128,1024]{1,0:T(8,128)S(1)} %add_half.3), channel_id=1, source_target_pairs={{0,48},{16,0},{32,16},{48,32},{1,49},{17,1},{33,17},{49,33},{2,50}... | collective-permute-start | bytes 1572872 | tf_op jit(solution)/shard_map/ppermute | solution.py:451
  19.4 13.2 %collective-permute-start.4 = (f32[128,1024]{1,0:T(8,128)S(1)}, f32[128,1024]{1,0:T(8,128)S(1)}, u32[]{:S(2)}, u32[]{:S(2)}) collective-permute-start(f32[128,1024]{1,0:T(8,128)S(1)} %add_half.2), channel_id=1, source_target_pairs={{0,16},{16,32},{32,48},{48,0},{1,17},{17,33},{33,49},{49,1},{2,18}... | collective-permute-start | bytes 1572872 | tf_op jit(solution)/shard_map/ppermute | solution.py:451
  20.1 10.5 %collective-permute-start.11 = (f32[256,128]{1,0:T(8,128)S(1)}, f32[256,128]{1,0:T(8,128)S(1)}, u32[]{:S(2)}, u32[]{:S(2)}) collective-permute-start(f32[256,128]{1,0:T(8,128)S(1)} %rows_of.1.b), channel_id=1, source_target_pairs={{0,4},{12,8},{17,21},{29,25},{34,38},{46,42},{51,55},{63,59},{64,6... | collective-permute-start | bytes 393224 | tf_op jit(solution)/shard_map/ppermute | solution.py:466
  31.2 3.2 %collective-permute-start.12 = (f32[256,128]{1,0:T(8,128)S(1)}, f32[256,128]{1,0:T(8,128)S(1)}, u32[]{:S(2)}, u32[]{:S(2)}) collective-permute-start(f32[256,128]{1,0:T(8,128)S(1)} %choose.3.b), channel_id=1, source_target_pairs={{0,2},{4,6},{12,14},{8,10},{17,19},{21,23},{29,31},{25,27},{34,36}... | collective-permute-start | bytes 393224 | tf_op jit(solution)/shard_map/ppermute | solution.py:466
  32.8 9.9 %collective-permute-start.8 = (f32[128,256]{1,0:T(8,128)S(1)}, f32[128,256]{1,0:T(8,128)S(1)}, u32[]{:S(2)}, u32[]{:S(2)}) collective-permute-start(f32[128,256]{1,0:T(8,128)S(1)} %get-tuple-element.69), channel_id=1, source_target_pairs={{0,64},{64,128},{128,192},{192,0},{1,65},{65,129},{129,193},{193,1... | collective-permute-start | bytes 393224 | tf_op jit(solution)/shard_map/ppermute | solution.py:451
  35.0 7.1 %collective-permute-start.13 = (f32[256,128]{1,0:T(8,128)S(1)}, f32[256,128]{1,0:T(8,128)S(1)}, u32[]{:S(2)}, u32[]{:S(2)}) collective-permute-start(f32[256,128]{1,0:T(8,128)S(1)} %choose.4.b), channel_id=1, source_target_pairs={{0,1},{2,3},{4,5},{6,7},{12,13},{14,15},{8,9},{10,11},{17,18},{19,... | collective-permute-start | bytes 393224 | tf_op jit(solution)/shard_map/ppermute | solution.py:466
  38.3 5.4 %collective-permute-start.9 = (f32[128,256]{1,0:T(8,128)S(1)}, f32[128,256]{1,0:T(8,128)S(1)}, u32[]{:S(2)}, u32[]{:S(2)}) collective-permute-start(f32[128,256]{1,0:T(8,128)S(1)} %get-tuple-element.70), channel_id=1, source_target_pairs={{0,128},{64,192},{128,0},{192,64},{1,129},{65,193},{129,1},{193,65... | collective-permute-start | bytes 393224 | tf_op jit(solution)/shard_map/ppermute | solution.py:451
  41.0 3.9 %collective-permute-start.10 = (f32[128,256]{1,0:T(8,128)S(1)}, f32[128,256]{1,0:T(8,128)S(1)}, u32[]{:S(2)}, u32[]{:S(2)}) collective-permute-start(f32[128,256]{1,0:T(8,128)S(1)} %get-tuple-element.71), channel_id=1, source_target_pairs={{0,192},{64,0},{128,64},{192,128},{1,193},{65,1},{129,65},{193,129... | collective-permute-start | bytes 393224 | tf_op jit(solution)/shard_map/ppermute | solution.py:451
  45.2 3.5 %collective-permute-start.16 = (f32[128,128]{1,0:T(8,128)S(1)}, f32[128,128]{1,0:T(8,128)S(1)}, u32[]{:S(2)}, u32[]{:S(2)}) collective-permute-start(f32[128,128]{1,0:T(8,128)S(1)} %get-tuple-element.73.refs_0_), channel_id=1, source_target_pairs={{0,48},{16,0},{32,16},{48,32},{1,49},{17,1},{33,17},{49,33},{2,50}... | collective-permute-start | bytes 196616 | tf_op jit(solution)/shard_map/ppermute | solution.py:451
  45.6 4.6 %collective-permute-start.15 = (f32[128,128]{1,0:T(8,128)S(1)}, f32[128,128]{1,0:T(8,128)S(1)}, u32[]{:S(2)}, u32[]{:S(2)}) collective-permute-start(f32[128,128]{1,0:T(8,128)S(1)} %get-tuple-element.73.refs_0_), channel_id=1, source_target_pairs={{0,32},{16,48},{32,0},{48,16},{1,33},{17,49},{33,1},{49,17},{2,34}... | collective-permute-start | bytes 196616 | tf_op jit(solution)/shard_map/ppermute | solution.py:451
  46.1 4.8 %collective-permute-start.14 = (f32[128,128]{1,0:T(8,128)S(1)}, f32[128,128]{1,0:T(8,128)S(1)}, u32[]{:S(2)}, u32[]{:S(2)}) collective-permute-start(f32[128,128]{1,0:T(8,128)S(1)} %get-tuple-element.73.refs_0_), channel_id=1, source_target_pairs={{0,16},{16,32},{32,48},{48,0},{1,17},{17,33},{33,49},{49,1},{2,18}... | collective-permute-start | bytes 196616 | tf_op jit(solution)/shard_map/ppermute | solution.py:451
  50.9 3.5 %collective-permute-start.19 = (f32[128,128]{1,0:T(8,128)S(1)}, f32[128,128]{1,0:T(8,128)S(1)}, u32[]{:S(2)}, u32[]{:S(2)}) collective-permute-start(f32[128,128]{1,0:T(8,128)S(1)} %total.3.refs_0_), channel_id=1, source_target_pairs={{0,192},{64,0},{128,64},{192,128},{1,193},{65,1},{129,65},{193,129... | collective-permute-start | bytes 196616 | tf_op jit(solution)/shard_map/ppermute | solution.py:451
  53.1 4.6 %collective-permute-start.18 = (f32[128,128]{1,0:T(8,128)S(1)}, f32[128,128]{1,0:T(8,128)S(1)}, u32[]{:S(2)}, u32[]{:S(2)}) collective-permute-start(f32[128,128]{1,0:T(8,128)S(1)} %total.3.refs_0_), channel_id=1, source_target_pairs={{0,128},{64,192},{128,0},{192,64},{1,129},{65,193},{129,1},{193,65... | collective-permute-start | bytes 196616 | tf_op jit(solution)/shard_map/ppermute | solution.py:451
  53.9 4.8 %collective-permute-start.17 = (f32[128,128]{1,0:T(8,128)S(1)}, f32[128,128]{1,0:T(8,128)S(1)}, u32[]{:S(2)}, u32[]{:S(2)}) collective-permute-start(f32[128,128]{1,0:T(8,128)S(1)} %total.3.refs_0_), channel_id=1, source_target_pairs={{0,64},{64,128},{128,192},{192,0},{1,65},{65,129},{129,193},{193,1... | collective-permute-start | bytes 196616 | tf_op jit(solution)/shard_map/ppermute | solution.py:451
  58.7 13.4 %collective-permute-start.20 = (f32[128,128]{1,0:T(8,128)S(1)}, f32[128,128]{1,0:T(8,128)S(1)}, u32[]{:S(2)}, u32[]{:S(2)}) collective-permute-start(f32[128,128]{1,0:T(8,128)S(1)} %total.4.refs_0_), channel_id=1, source_target_pairs={{0,8},{8,0},{1,9},{9,1},{2,10},{10,2},{3,11},{11,3},{4,12},{12,4},... | collective-permute-start | bytes 196616 | tf_op jit(solution)/shard_map/ppermute | solution.py:451
  97.1 3.9 %collective-permute-start.23 = (f32[256,128]{1,0:T(8,128)S(1)}, f32[256,128]{1,0:T(8,128)S(1)}, u32[]{:S(2)}, u32[]{:S(2)}) collective-permute-start(f32[256,128]{1,0:T(8,128)S(1)} %get-tuple-element.74.refs_0_), channel_id=1, source_target_pairs={{0,192},{64,0},{128,64},{192,128},{1,193},{65,1},{129,65},{193,129... | collective-permute-start | bytes 393224 | tf_op jit(solution)/shard_map/ppermute | solution.py:451
  97.1 5.5 %collective-permute-start.22 = (f32[256,128]{1,0:T(8,128)S(1)}, f32[256,128]{1,0:T(8,128)S(1)}, u32[]{:S(2)}, u32[]{:S(2)}) collective-permute-start(f32[256,128]{1,0:T(8,128)S(1)} %get-tuple-element.74.refs_0_), channel_id=1, source_target_pairs={{0,128},{64,192},{128,0},{192,64},{1,129},{65,193},{129,1},{193,65... | collective-permute-start | bytes 393224 | tf_op jit(solution)/shard_map/ppermute | solution.py:451
  98.1 5.8 %collective-permute-start.21 = (f32[256,128]{1,0:T(8,128)S(1)}, f32[256,128]{1,0:T(8,128)S(1)}, u32[]{:S(2)}, u32[]{:S(2)}) collective-permute-start(f32[256,128]{1,0:T(8,128)S(1)} %get-tuple-element.74.refs_0_), channel_id=1, source_target_pairs={{0,64},{64,128},{128,192},{192,0},{1,65},{65,129},{129,193},{193,1... | collective-permute-start | bytes 393224 | tf_op jit(solution)/shard_map/ppermute | solution.py:451
  104.0 16.6 %collective-permute-start.26 = (f32[1024,128]{1,0:T(8,128)S(1)}, f32[1024,128]{1,0:T(8,128)S(1)}, u32[]{:S(2)}, u32[]{:S(2)}) collective-permute-start(f32[1024,128]{1,0:T(8,128)S(1)} %stack.22.refs_0_.refs_17_), channel_id=1, source_target_pairs={{0,48},{16,0},{32,16},{48,32},{1,49},{17,1},{33,17},{49,33},{2,50}... | collective-permute-start | bytes 1572872 | tf_op jit(solution)/shard_map/ppermute | solution.py:451
  104.7 15.9 %collective-permute-start.25 = (f32[1024,128]{1,0:T(8,128)S(1)}, f32[1024,128]{1,0:T(8,128)S(1)}, u32[]{:S(2)}, u32[]{:S(2)}) collective-permute-start(f32[1024,128]{1,0:T(8,128)S(1)} %stack.22.refs_0_.refs_17_), channel_id=1, source_target_pairs={{0,16},{16,32},{32,48},{48,0},{1,17},{17,33},{33,49},{49,1},{2,18}... | collective-permute-start | bytes 1572872 | tf_op jit(solution)/shard_map/ppermute | solution.py:451
  105.6 11.6 %collective-permute-start.24 = (f32[1024,128]{1,0:T(8,128)S(1)}, f32[1024,128]{1,0:T(8,128)S(1)}, u32[]{:S(2)}, u32[]{:S(2)}) collective-permute-start(f32[1024,128]{1,0:T(8,128)S(1)} %stack.22.refs_0_.refs_17_), channel_id=1, source_target_pairs={{0,8},{8,0},{1,9},{9,1},{2,10},{10,2},{3,11},{11,3},{4,12},{12,4},... | collective-permute-start | bytes 1572872 | tf_op jit(solution)/shard_map/ppermute | solution.py:451
  120.6 3.4 %collective-permute-start.28 = (f32[1024,128]{1,0:T(8,128)S(1)}, f32[1024,128]{1,0:T(8,128)S(1)}, u32[]{:S(2)}, u32[]{:S(2)}) collective-permute-start(f32[1024,128]{1,0:T(8,128)S(1)} %collective-permute-done.25.refs_0_.a_ref.refs_19_), channel_id=1, source_target_pairs={{0,8},{8,0},{1,9},{9,1},{2,10},{10,2},{3,11},{11,3},{4,12},{12,4},... | collective-permute-start | bytes 1572872 | tf_op jit(solution)/shard_map/ppermute | solution.py:451
  120.7 6.7 %collective-permute-start.27 = (f32[1024,128]{1,0:T(8,128)S(1)}, f32[1024,128]{1,0:T(8,128)S(1)}, u32[]{:S(2)}, u32[]{:S(2)}) collective-permute-start(f32[1024,128]{1,0:T(8,128)S(1)} %collective-permute-done.26.refs_0_.b_ref.refs_21_), channel_id=1, source_target_pairs={{0,8},{8,0},{1,9},{9,1},{2,10},{10,2},{3,11},{11,3},{4,12},{12,4},... | collective-permute-start | bytes 1572872 | tf_op jit(solution)/shard_map/ppermute | solution.py:451
  121.2 9.5 %collective-permute-start.29 = (f32[512,128]{1,0:T(8,128)S(1)}, f32[512,128]{1,0:T(8,128)S(1)}, u32[]{:S(2)}, u32[]{:S(2)}) collective-permute-start(f32[512,128]{1,0:T(8,128)S(1)} %get-tuple-element.97), channel_id=1, source_target_pairs={{0,16},{16,32},{32,48},{48,0},{1,17},{17,33},{33,49},{49,1},{2,18}... | collective-permute-start | bytes 786440 | tf_op jit(solution)/shard_map/ppermute | solution.py:451
  121.3 9.4 %collective-permute-start.30 = (f32[512,128]{1,0:T(8,128)S(1)}, f32[512,128]{1,0:T(8,128)S(1)}, u32[]{:S(2)}, u32[]{:S(2)}) collective-permute-start(f32[512,128]{1,0:T(8,128)S(1)} %get-tuple-element.98), channel_id=1, source_target_pairs={{0,48},{16,0},{32,16},{48,32},{1,49},{17,1},{33,17},{49,33},{2,50}... | collective-permute-start | bytes 786440 | tf_op jit(solution)/shard_map/ppermute | solution.py:451
  130.8 2.3 %collective-permute-start.31 = (f32[1024,128]{1,0:T(8,128)S(1)}, f32[1024,128]{1,0:T(8,128)S(1)}, u32[]{:S(2)}, u32[]{:S(2)}) collective-permute-start(f32[1024,128]{1,0:T(8,128)S(1)} %stack.23.refs_0_), channel_id=1, source_target_pairs={{0,8},{8,0},{1,9},{9,1},{2,10},{10,2},{3,11},{11,3},{4,12},{12,4},... | collective-permute-start | bytes 1572872 | tf_op jit(solution)/shard_map/ppermute | solution.py:451
  (5 other events, 41.0 us)
